TPU v7x, 32 devices: a whole 2x2x4 slice. The times are simulated.
32 devices in a mesh: dp: 4 (over y, x), fsdp: 8 (over z, core).
Axes of the slice: x: 2, y: 2, z: 4, core: 2. Of those that a mesh axis runs over, the one named last changes fastest.
Arguments:
- features: bfloat16 [128, 2, 10, 10, 768], P(('dp', 'fsdp')), may hold values from -6 to 6
- cotangent: bfloat16 [128, 2, 10, 10, 768], P(('dp', 'fsdp')), may hold values from -6 to 6
- image_sizes: int32 [128], P(('dp', 'fsdp')), may hold values from 0 to 10, as said below
- warp_index: int32 [128, 100, 4], P(('dp', 'fsdp')), may hold values from 0 to 99, as said below
- warp_weight: float32 [128, 100, 4], P(('dp', 'fsdp')), may hold values from 0 to 1, as said below
- offsets: int32 [81, 2], replicated, may hold values from -4 to 4, as said below
- conv_kernel: bfloat16 [49, 768], P(None, 'fsdp'), may hold values from -0.875 to 0.875
- conv_bias: bfloat16 [768], P('fsdp'), may hold values from -3 to 3
- norm_gain: bfloat16 [768], P('fsdp'), may hold values from 0.5 to 1.5
- norm_bias: bfloat16 [768], P('fsdp'), may hold values from -2 to 2
- w_in: bfloat16 [768, 3072], P('fsdp'), may hold values from -0.21875 to 0.21875
- bias_in: bfloat16 [3072], P('fsdp'), may hold values from -2 to 2
- w_out: bfloat16 [3072, 768], P('fsdp'), may hold values from -0.109375 to 0.109375
- bias_out: bfloat16 [768], P('fsdp'), may hold values from -2 to 2
- layer_scale: bfloat16 [768], P('fsdp'), may hold values from 0.5 to 1.5
- w_estimate: bfloat16 [81, 768], P(None, 'fsdp'), may hold values from -0.625 to 0.625
Outputs:
- mixed_out: bfloat16 [128, 2, 10, 10, 768], P(('dp', 'fsdp'))
- grad_features: float32 [128, 2, 10, 10, 768], P(('dp', 'fsdp'))
- grad_conv_kernel: float32 [49, 768], P(None, 'fsdp')
- grad_conv_bias: float32 [768], P('fsdp')
- grad_norm_gain: float32 [768], P('fsdp')
- grad_norm_bias: float32 [768], P('fsdp')
- grad_w_in: float32 [768, 3072], P('fsdp')
- grad_bias_in: float32 [3072], P('fsdp')
- grad_w_out: float32 [3072, 768], P('fsdp')
- grad_bias_out: float32 [768], P('fsdp')
- grad_layer_scale: float32 [768], P('fsdp')
- grad_w_estimate: float32 [81, 768], P(None, 'fsdp')
Inputs may be any that keep to these rules, and one draw needn't show every extreme that they name: `image_sizes`: each value is 0, 7, 8 or 10; in each device's 4 slots the live images come first and empty slots (0) last, and some device has no empty slot. `warp_index`: cells of the same slot; inside the image, the four corners of a unit square that lies in the image; outside it, the cell itself four times. `warp_weight`: nonnegative bilinear weights, four to a cell, summing to one. `offsets`: the rows are the 81 cells of a 9 x 9 window centred at zero, each once, in some order.
All inputs are finite; a program needn't handle non-finite values.
Results may differ from a plain program's by a relative error of at most 0.0072.
Values may be sent and summed in bfloat16 or wider, within the bound.
No kernel may reach another device: no remote copies, remote signals or barrier semaphores. Data moves between devices by JAX's collectives and lax.ppermute only.
A program may use at most 320 MiB of HBM per device.

v0:
```python
import jax
import jax.numpy as jnp
from jax import lax
from jax.sharding import PartitionSpec as P

CANVAS = 10
KERNEL = 7
PIX = 100


EPSILON = 1e-06
HIGHEST = lax.Precision.HIGHEST


def gelu_exact(values):
    return jax.nn.gelu(values, approximate=False)


def pixel_mask(image_sizes):
    places = jnp.arange(CANVAS, dtype=jnp.int32)
    inside = places[None, :] < image_sizes[:, None]
    return (inside[:, :, None] & inside[:, None, :]).astype(jnp.float32)


def warp_matrix(warp_index, warp_weight):
    cells = jnp.arange(PIX, dtype=jnp.int32)
    onehot = (warp_index[..., None] == cells).astype(jnp.float32)
    return jnp.sum(warp_weight[..., None] * onehot, axis=2)


def select_table(offsets):
    cells = jnp.arange(PIX, dtype=jnp.int32)
    row_of = cells // CANVAS
    col_of = cells % CANVAS
    target_row = row_of[:, None] + offsets[None, :, 0]
    target_col = col_of[:, None] + offsets[None, :, 1]
    valid = (target_row >= 0) & (target_row < CANVAS) & (target_col >= 0) & (target_col < CANVAS)
    target = target_row * CANVAS + target_col
    return (valid[..., None] & (target[..., None] == cells)).astype(jnp.float32)


def depthwise(images_flat, kernel):
    reach = KERNEL // 2
    padded = jnp.pad(images_flat, ((0, 0), (reach, reach), (reach, reach), (0, 0)))
    total = jnp.zeros(images_flat.shape, images_flat.dtype)
    for row_tap in range(KERNEL):
        for col_tap in range(KERNEL):
            total = (
                total
                + padded[:, row_tap : row_tap + CANVAS, col_tap : col_tap + CANVAS, :]
                * kernel[row_tap * KERNEL + col_tap]
            )
    return total


def mix_norm(images_flat, kernel, conv_bias, norm_gain, norm_bias):
    conv_out = depthwise(images_flat, kernel) + conv_bias
    rows_in = conv_out.reshape(-1, conv_out.shape[-1])
    centred = rows_in - jnp.mean(rows_in, axis=-1, keepdims=True)
    variance = jnp.mean(centred * centred, axis=-1, keepdims=True)
    return centred * lax.rsqrt(variance + EPSILON) * norm_gain + norm_bias


def shards(
    features,
    cotangent,
    image_sizes,
    warp_index,
    warp_weight,
    offsets,
    conv_kernel,
    conv_bias,
    norm_gain,
    norm_bias,
    w_in,
    bias_in,
    w_out,
    bias_out,
    layer_scale,
    w_estimate,
):
    gathered = (
        lax.all_gather(conv_kernel, "fsdp", axis=1, tiled=True),
        lax.all_gather(conv_bias, "fsdp", axis=0, tiled=True),
        lax.all_gather(norm_gain, "fsdp", axis=0, tiled=True),
        lax.all_gather(norm_bias, "fsdp", axis=0, tiled=True),
        lax.all_gather(w_in, "fsdp", axis=0, tiled=True),
        lax.all_gather(bias_in, "fsdp", axis=0, tiled=True),
        lax.all_gather(w_out, "fsdp", axis=0, tiled=True),
        lax.all_gather(bias_out, "fsdp", axis=0, tiled=True),
        lax.all_gather(layer_scale, "fsdp", axis=0, tiled=True),
        lax.all_gather(w_estimate, "fsdp", axis=1, tiled=True),
    )
    (
        kernel_all,
        conv_bias_all,
        gain_all,
        shift_all,
        win_all,
        bin_all,
        wout_all,
        bout_all,
        scale_all,
        west_all,
    ) = gathered
    images_here = features.shape[0]
    channels = features.shape[-1]
    side_mask = pixel_mask(image_sizes)
    frame_mask = jnp.broadcast_to(side_mask[:, None], (images_here, 2, CANVAS, CANVAS)).reshape(
        -1, 1
    )
    pixel_rows = side_mask.reshape(images_here, PIX, 1)
    inputs = features.astype(jnp.float32) * side_mask[:, None, :, :, None]
    normed, pull_norm = jax.vjp(
        mix_norm,
        inputs.reshape(-1, CANVAS, CANVAS, channels),
        kernel_all.astype(jnp.float32),
        conv_bias_all.astype(jnp.float32),
        gain_all.astype(jnp.float32),
        shift_all.astype(jnp.float32),
    )
    normed_low = normed.astype(jnp.bfloat16)
    hidden = jnp.dot(normed_low, win_all, preferred_element_type=jnp.float32) + bin_all.astype(
        jnp.float32
    )
    active, pull_active = jax.vjp(gelu_exact, hidden)
    active_low = active.astype(jnp.bfloat16)
    branch = jnp.dot(active_low, wout_all, preferred_element_type=jnp.float32) + bout_all.astype(
        jnp.float32
    )
    mixed = (inputs.reshape(-1, channels) + scale_all.astype(jnp.float32) * branch) * frame_mask
    mixed_frames = mixed.reshape(images_here, 2, PIX, channels)
    first = mixed_frames[:, 0]
    second = mixed_frames[:, 1]
    mats = warp_matrix(warp_index, warp_weight)
    table = select_table(offsets)
    second_low = second.astype(jnp.bfloat16)
    warped = jnp.einsum("npq,nqd->npd", mats, second_low.astype(jnp.float32), precision=HIGHEST)
    warped_low = warped.astype(jnp.bfloat16)
    first_low = first.astype(jnp.bfloat16)
    scores = jnp.einsum("npd,nqd->npq", first_low, warped_low, preferred_element_type=jnp.float32)
    cost = jnp.einsum("npq,pkq->npk", scores, table, precision=HIGHEST) * channels ** (-0.5)
    gated, pull_gated = jax.vjp(gelu_exact, cost)
    gated_low = gated.astype(jnp.bfloat16)
    head = jnp.einsum("npk,kd->npd", gated_low, west_all, preferred_element_type=jnp.float32)
    first_out = (first + head) * pixel_rows
    mixed_out = jnp.stack([first_out, second], axis=1).reshape(features.shape).astype(jnp.bfloat16)
    win_back, wout_back, scale_back, west_back = (
        lax.all_gather(w_in, "fsdp", axis=0, tiled=True),
        lax.all_gather(w_out, "fsdp", axis=0, tiled=True),
        lax.all_gather(layer_scale, "fsdp", axis=0, tiled=True),
        lax.all_gather(w_estimate, "fsdp", axis=1, tiled=True),
    )
    upstream = cotangent.astype(jnp.float32).reshape(images_here, 2, PIX, channels)
    d_first = upstream[:, 0] * pixel_rows
    d_head_low = d_first.astype(jnp.bfloat16)
    grad_west = jnp.einsum("npk,npd->kd", gated_low, d_head_low, preferred_element_type=jnp.float32)
    d_gated = jnp.einsum("npd,kd->npk", d_head_low, west_back, preferred_element_type=jnp.float32)
    (d_cost,) = pull_gated(d_gated)
    d_scores_low = (
        jnp.einsum("npk,pkq->npq", d_cost, table, precision=HIGHEST) * channels ** (-0.5)
    ).astype(jnp.bfloat16)
    d_first = d_first + jnp.einsum(
        "npq,nqd->npd", d_scores_low, warped_low, preferred_element_type=jnp.float32
    )
    d_warped_low = jnp.einsum(
        "npq,npd->nqd", d_scores_low, first_low, preferred_element_type=jnp.float32
    ).astype(jnp.bfloat16)
    d_second = upstream[:, 1] + jnp.einsum(
        "npq,npd->nqd", mats, d_warped_low.astype(jnp.float32), precision=HIGHEST
    )
    d_mixed = jnp.stack([d_first, d_second], axis=1).reshape(-1, channels) * frame_mask
    grad_scale = jnp.sum(d_mixed * branch, axis=0)
    d_branch_low = (d_mixed * scale_back.astype(jnp.float32)).astype(jnp.bfloat16)
    grad_bout = jnp.sum(d_branch_low.astype(jnp.float32), axis=0)
    grad_wout = jnp.einsum(
        "rf,rd->fd", active_low, d_branch_low, preferred_element_type=jnp.float32
    )
    d_active = jnp.einsum("rd,fd->rf", d_branch_low, wout_back, preferred_element_type=jnp.float32)
    (d_hidden,) = pull_active(d_active)
    d_hidden_low = d_hidden.astype(jnp.bfloat16)
    grad_bin = jnp.sum(d_hidden_low.astype(jnp.float32), axis=0)
    grad_win = jnp.einsum("rd,rf->df", normed_low, d_hidden_low, preferred_element_type=jnp.float32)
    d_normed = jnp.einsum("rf,df->rd", d_hidden_low, win_back, preferred_element_type=jnp.float32)
    d_images, grad_kernel, grad_cbias, grad_gain, grad_shift = pull_norm(d_normed)
    grad_features = ((d_mixed + d_images.reshape(-1, channels)) * frame_mask).reshape(
        features.shape
    )
    summed = (
        lax.psum_scatter(grad_kernel, "fsdp", scatter_dimension=1, tiled=True),
        lax.psum_scatter(grad_cbias, "fsdp", scatter_dimension=0, tiled=True),
        lax.psum_scatter(grad_gain, "fsdp", scatter_dimension=0, tiled=True),
        lax.psum_scatter(grad_shift, "fsdp", scatter_dimension=0, tiled=True),
        lax.psum_scatter(grad_win, "fsdp", scatter_dimension=0, tiled=True),
        lax.psum_scatter(grad_bin, "fsdp", scatter_dimension=0, tiled=True),
        lax.psum_scatter(grad_wout, "fsdp", scatter_dimension=0, tiled=True),
        lax.psum_scatter(grad_bout, "fsdp", scatter_dimension=0, tiled=True),
        lax.psum_scatter(grad_scale, "fsdp", scatter_dimension=0, tiled=True),
        lax.psum_scatter(grad_west, "fsdp", scatter_dimension=1, tiled=True),
    )
    (
        part_kernel,
        part_cbias,
        part_gain,
        part_shift,
        part_win,
        part_bin,
        part_wout,
        part_bout,
        part_scale,
        part_west,
    ) = summed
    totals = lax.psum(
        (
            part_kernel,
            part_cbias,
            part_gain,
            part_shift,
            part_win,
            part_bin,
            part_wout,
            part_bout,
            part_scale,
            part_west,
        ),
        "dp",
    )
    return (
        mixed_out,
        grad_features,
        totals[0],
        totals[1],
        totals[2],
        totals[3],
        totals[4],
        totals[5],
        totals[6],
        totals[7],
        totals[8],
        totals[9],
    )


def solution(mesh):
    in_specs = (
        P(("dp", "fsdp"), None, None, None, None),
        P(("dp", "fsdp"), None, None, None, None),
        P(("dp", "fsdp")),
        P(("dp", "fsdp"), None, None),
        P(("dp", "fsdp"), None, None),
        P(),
        P(None, "fsdp"),
        P("fsdp"),
        P("fsdp"),
        P("fsdp"),
        P("fsdp", None),
        P("fsdp"),
        P("fsdp", None),
        P("fsdp"),
        P("fsdp"),
        P(None, "fsdp"),
    )
    out_specs = (
        P(("dp", "fsdp"), None, None, None, None),
        P(("dp", "fsdp"), None, None, None, None),
        P(None, "fsdp"),
        P("fsdp"),
        P("fsdp"),
        P("fsdp"),
        P("fsdp", None),
        P("fsdp"),
        P("fsdp", None),
        P("fsdp"),
        P("fsdp"),
        P(None, "fsdp"),
    )
    return jax.shard_map(shards, mesh=mesh, in_specs=in_specs, out_specs=out_specs, check_vma=False)
```

profile of v0, /device:TPU:0, one launch (start us, length us, event | category | flops | bytes accessed | tf_op | source)
XLA Modules:
  0.0 581.2 jit_solution(5525770775088591213)
XLA Ops:
  9.8 16.0 %all-gather = bf16[8,96,49]{1,2,0:T(8,128)(2,1)S(1)} all-gather(bf16[1,96,49]{1,2,0:T(8,128)(2,1)} %bitcast.167), channel_id=1, replica_groups=mesh['dp'=4,'fsdp'=8] {'fsdp'}, dimensions={0}, use_global_device_ids=true | all-gather | bytes 84672 | tf_op jit(solution)/shard_map/all_gather | solution.py:83
  27.8 3.3 copy.563
  31.1 2.5 copy.562
  36.1 30.2 %all-reduce.113 = (bf16[768]{0:T(1024)(128)(2,1)S(1)}, bf16[768]{0:T(1024)(128)(2,1)S(1)}, bf16[768]{0:T(1024)(128)(2,1)S(1)}, bf16[768]{0:T(1024)(128)(2,1)S(1)}, bf16[768]{0:T(1024)(128)(2,1)S(1)}) all-reduce(bf16[768]{0:T(1024)(128)(2,1)S(1)} %dynamic-update-slice.1, ...), channel_id=1, replica_groups=mesh['dp'=4,'fsdp'=8] {'fsdp'}, use_global_device_ids=true, to_apply=%add.100 | all-reduce | flops 3840 | bytes 15360
  66.3 3.2 reshape.592
  69.8 17.7 %fusion.71 = (f32[8,10,10]{0,2,1:T(8,128)S(1)}, f32[8,10,10,768]{3,0,2,1:T(8,128)}) fusion(f32[768]{0:T(1024)S(1)} %convert_element_type.107, f32[768]{0:T(1024)S(1)} %get-tuple-element.124, f32[768]{0:T(1024)S(1)} %get-tuple-element.125, f32[768]{0:T(1024)} %get-tuple-element.126, f32[768]{0:T(1024)} %get-tuple-element.127, f32[768]{0:T(1024)} %get-tuple-element.128, ...), kind=kLoop, calls=%fused_computation.330 | loop fusion | flops 60824800 | bytes 5072000 | tf_op jit(solution)/shard_map/jvp()/reduce_sum | solution.py:59
  87.7 2.3 multiply_reduce_fusion.51
  90.0 2.8 copy.565
  92.9 13.2 %all-gather.1 = bf16[8,1,384]{2,1,0:T(2,128)(2,1)S(1)} all-gather(bf16[1,1,384]{2,1,0:T(2,128)(2,1)S(1)} %reshape.621), channel_id=1, replica_groups=mesh['dp'=4,'fsdp'=8] {'fsdp'}, dimensions={0}, use_global_device_ids=true | all-gather | bytes 6912 | tf_op jit(solution)/shard_map/all_gather | solution.py:88
  106.3 14.5 %all-gather.2 = bf16[8,96,81]{1,2,0:T(8,128)(2,1)S(1)} all-gather(bf16[1,96,81]{1,2,0:T(8,128)(2,1)S(1)} %bitcast.166), channel_id=1, replica_groups=mesh['dp'=4,'fsdp'=8] {'fsdp'}, dimensions={0}, use_global_device_ids=true | all-gather | bytes 139968 | tf_op jit(solution)/shard_map/all_gather | solution.py:92
  121.3 4.4 reshape.591
  126.2 2.9 reshape.593
  129.4 5.4 fusion.72
  134.9 1.0 copy-done.8
  135.9 1.1 fusion.39
  137.0 1.2 select_reduce_fusion
  138.2 29.2 %multiply_convert_fusion = (bf16[800,3072]{1,0:T(8,128)(2,1)}, f32[800,3072]{1,0:T(8,128)}, f32[800,3072]{1,0:T(8,128)}) fusion(f32[3072]{0:T(1024)S(1)} %bitcast.168, bf16[768,3072]{1,0:T(8,128)(2,1)} %all-gather.6.cloned.1.call-done, f32[800,768]{1,0:T(8,128)S(1)} %reshape.593, f32[768]{0:T(1024)S(1)} %convert_element_type.109, ...), kind=kOutput, calls=%fused_computation.52 | convolution fusion | flops 3940147200 | bytes 31777024 | tf_op jit(solution)/shard_map/dot_general | solution.py:123
  167.5 10.8 %add_multiply_fusion = (f32[800,768]{1,0:T(8,128)}, f32[800,768]{1,0:T(8,128)}) fusion(f32[800,768]{1,0:T(8,128)} %reshape.591, f32[800]{0:T(1024)S(1)} %mul.1320, f32[768]{0:T(1024)S(1)} %convert_element_type.113, f32[768]{0:T(1024)S(1)} %convert_element_type.105, bf16[800,3072]{1,0:T(8,128)(2,1)} %get-tuple-element.200, ...), kind=kOutput, calls=%fused_computation.138 | convolution fusion | flops 3777331200 | bytes 17015936 | tf_op jit(solution)/shard_map/dot_general | solution.py:128
  178.3 1.8 reshape.594
  181.1 7.2 %fusion.9 = f32[100,81,4]{1,2,0:T(4,128)} fusion(s32[100,81]{1,0:T(8,128)S(1)} %add_add_fusion.2, pred[100,81]{1,0:T(8,128)(4,1)S(1)} %fusion.62, f32[4,100,100]{2,1,0:T(8,128)S(1)} %fusion.35), kind=kOutput, calls=%fused_computation.70 | convolution fusion | flops 40500000 | bytes 330100 | tf_op jit(solution)/shard_map/npq,pkq->npk/dot_general | solution.py:142
  188.3 1.7 copy.573
  190.1 2.5 fusion.49
  192.6 1.7 copy.582
  194.3 6.0 %fusion.30 = bf16[4,100,100]{2,0,1:T(4,128)(2,1)} fusion(f32[4,100,81]{2,0,1:T(4,128)} %copy.582, s32[100,81]{1,0:T(8,128)S(1)} %add_add_fusion.2, pred[100,81]{1,0:T(8,128)(4,1)S(1)} %fusion.62), kind=kOutput, calls=%fused_computation.216 | convolution fusion | flops 40580000 | bytes 250100 | tf_op jit(solution)/shard_map/npk,pkq->npq/dot_general | solution.py:161
  200.3 1.1 copy.586
  201.3 1.8 convolution_add_fusion
  204.3 1.0 convert_reduce_fusion.1
  205.5 1.6 reshape.597
  207.1 14.5 %convert_reduce_fusion = (f32[3072]{0:T(1024)}, bf16[800,3072]{1,0:T(8,128)(2,1)S(1)}) fusion(f32[800,3072]{1,0:T(8,128)} %get-tuple-element.201, bf16[3072,768]{1,0:T(8,128)(2,1)} %all-gather.8.cloned.1.call-done, f32[800,768]{1,0:T(8,128)} %reshape.597, f32[800]{0:T(1024)S(1)} %mul.1320, f32[768]{0:T(1024)S(1)} %convert_element_type.105, ...), kind=kOutput, calls=%fused_computation.50 | convolution fusion | flops 3818492928 | bytes 31783040 | tf_op jit(solution)/shard_map/rd,fd->rf/dot_general | solution.py:179
  221.6 2.1 copy-done.18
  223.8 8.5 %fusion.65 = f32[768,3072]{1,0:T(8,128)} fusion(bf16[800,3072]{1,0:T(8,128)(2,1)S(1)} %get-tuple-element.268, f32[800,768]{1,0:T(8,128)S(1)} %copy-done.7, f32[768]{0:T(1024)S(1)} %convert_element_type.109, f32[768]{0:T(1024)S(1)} %convert_element_type.108, f32[800]{0:T(1024)S(1)} %rsqrt.10, f32[800]{0:T(1024)S(1)} %div.31), kind=kOutput, calls=%fused_computation.326 | convolution fusion | flops 3777945600 | bytes 16822528 | tf_op jit(solution)/shard_map/rd,rf->df/dot_general | solution.py:183
  232.4 10.2 %fusion.63 = f32[3072,768]{1,0:T(8,128)} fusion(bf16[800,3072]{1,0:T(8,128)(2,1)} %get-tuple-element.200, f32[800,768]{1,0:T(8,128)} %reshape.597, f32[800]{0:T(1024)S(1)} %mul.1320, f32[768]{0:T(1024)S(1)} %convert_element_type.105), kind=kOutput, calls=%fused_computation.324 | convolution fusion | flops 3776716800 | bytes 16816256 | tf_op jit(solution)/shard_map/rf,rd->fd/dot_general | solution.py:176
  242.7 2.9 copy.588
  245.6 1.5 copy.584
  247.1 9.0 %multiply_reduce_fusion.1 = (f32[768]{0:T(1024)}, f32[800]{0:T(1024)S(1)}, f32[768]{0:T(1024)}, f32[800,768]{1,0:T(8,128)S(1)}) fusion(f32[800,768]{1,0:T(8,128)S(1)} %copy-done.7, f32[800]{0:T(1024)S(1)} %rsqrt.10, f32[800]{0:T(1024)S(1)} %div.31, f32[768]{0:T(1024)S(1)} %convert_element_type.108, bf16[800,3072]{1,0:T(8,128)(2,1)} %copy-done.18, ...), kind=kOutput, calls=%fused_computation.87 | convolution fusion | flops 3779786496 | bytes 14567808 | tf_op jit(solution)/shard_map/rf,df->rd/dot_general | solution.py:184
  256.1 0.9 fusion.68
  257.9 1.5 copy-done.5
  259.4 2.3 reshape.600
  261.7 4.3 reshape.598
  266.0 5.7 multiply_reduce_fusion.47
  278.8 3.9 multiply_reduce_fusion.49
  283.3 4.6 multiply_reduce_fusion.48
  308.5 9.2 %broadcast_multiply_fusion.2 = (f32[8,10,10,768]{3,0,2,1:T(8,128)S(1)}, f32[8,10,10,768]{3,0,2,1:T(8,128)S(1)}, f32[8,10,10,768]{3,0,2,1:T(8,128)S(1)}, f32[8,10...) fusion(f32[8,10,10,768]{3,0,2,1:T(8,128)S(1)} %get-tuple-elemen, ...), kind=kLoop, calls=%fused_computation.164 | loop fusion | flops 7987200 | bytes 34446336 | tf_op jit(solution)/shard_map/transpose(jvp())/mul | solution.py:50
  317.8 15.2 %broadcast_multiply_fusion.1 = (f32[8,10,10,768]{3,0,2,1:T(8,128)}, f32[8,10,10,768]{3,0,2,1:T(8,128)}, f32[8,10,10,768]{3,0,2,1:T(8,128)}, f32[8,10,10,768]{3,0...) fusion(f32[8,10,10,768]{3,0,2,1:T(8,128)S(1)} %get-tuple-elemen, ...), kind=kLoop, calls=%fused_computation.163 | loop fusion | flops 11059200 | bytes 46749696 | tf_op jit(solution)/shard_map/transpose(jvp())/mul | solution.py:50
  333.2 15.4 %broadcast_multiply_fusion = (f32[8,10,10,768]{3,0,2,1:T(8,128)}, f32[8,10,10,768]{3,0,2,1:T(8,128)}, f32[8,10,10,768]{3,0,2,1:T(8,128)}, f32[8,10,10,768]{3,0,2...) fusion(f32[8,10,10,768]{3,0,2,1:T(8,128)S(1)} %get-tuple-elemen, ...), kind=kLoop, calls=%fused_computation.162 | loop fusion | flops 11059200 | bytes 46749696 | tf_op jit(solution)/shard_map/transpose(jvp())/mul | solution.py:50
  348.7 45.1 %pad_add_fusion = f32[8,16,16,768]{3,0,2,1:T(8,128)S(1)} fusion(f32[8,10,10,768]{3,0,2,1:T(8,128)} %get-tuple-element.213, f32[8,10,10,768]{3,0,2,1:T(8,128)} %get-tuple-element.214, f32[8,10,10,768]{3,0,2,1:T(8,128)} %get-tuple-element.215, f32[8,10,10,768]{3,0,2,1:T(8,128)} %get-tuple-element.216, f32[8,10,10,768]{3,0,2,1:T(8,128)} %get-tuple-element.217, ...), kind=kLoop, calls=%fused_computation.66 | loop fusion | flops 66060288 | bytes 111968256 | tf_op jit(solution)/shard_map/transpose(jvp())/add_any | solution.py:50
  393.8 4.0 pad_add_fusion.1
  397.8 2.5 reshape.599
  400.7 8.7 %fusion.13 = (f32[768]{0:T(1024)S(1)}, f32[4,2,10,10,768]{4,0,3,2,1:T(4,128)}) fusion(f32[4,2,10,10,768]{4,3,2,1,0:T(8,128)} %reshape.600, f32[4,10,10]{0,2,1:T(8,128)S(1)} %copy-done.25, bf16[4,2,10,10,768]{4,1,3,2,0:T(2,128)(2,1)} %param.16, f32[4,2,10,10,768]{4,1,0,3,2:T(2,128)} %reshape.599, f32[4,1,10,10,768]{4,0,3,2,1:T(4,128)} %bitcast.156, ...), kind=kLoop, calls=%fused_computation.85 | loop fusion | flops 4914432 | bytes 11063872 | tf_op jit(solution)/shard_map/transpose(jvp())/reduce_sum | solution.py:50
  409.7 1.1 pad_add_fusion.7
  410.8 0.9 copy.693
  412.0 2.8 convolution_bitcast_fusion
  414.8 15.6 %reduce-scatter.11.cloned.1.call-done = f32[384,768]{1,0:T(8,128)} async-done(((f32[3072,768]{1,0:T(8,128)}), f32[384,768]{1,0:T(8,128)}) %reduce-scatter.11.cloned.1.call-update) | async-done | bytes 1179664 | tf_op jit(solution)/shard_map/reduce_scatter | solution.py:196
  432.7 0.9 pad_maximum_fusion.1
  433.6 2.0 copy.690
  436.3 26.2 %all-reduce.110 = (f32[768]{0:T(1024)S(1)}, f32[768]{0:T(1024)S(1)}, f32[768]{0:T(1024)S(1)}, f32[3072]{0:T(1024)S(1)}, f32[768]{0:T(1024)S(1)}, /*index=5*/f32[768]{0:T(1024)S(1)}) all-reduce(f32[768]{0:T(1024)S(1)} %copy-done.86, f32[768]{0:T(1024)S(1)} %copy-done.130, ...), channel_id=3, replica_groups=mesh['dp'=4,'fsdp'=8] {'fsdp'}, use_global_device_ids=true, to_apply=%region_57.58.clone | all-reduce | flops 6912 | bytes 55296
  462.9 3.3 copy.691
  466.3 0.9 copy.694
  467.2 26.5 %reduce-scatter.15.cloned.1.call-done = f32[96,81]{1,0:T(8,128)} async-done(((f32[768,81]{1,0:T(8,128)}), f32[96,81]{1,0:T(8,128)}) %reduce-scatter.15.cloned.1.call-update) | async-done | bytes 31120
  493.7 0.9 copy.696
  494.6 19.2 %all-reduce.111 = (f32[49,96]{1,0:T(8,128)}, f32[96]{0:T(128)}, f32[96]{0:T(128)}, f32[96]{0:T(128)}, f32[384]{0:T(512)}, /*index=5*/f32[96]{0:T(128)}, f32[96]{0:T(128)}, f32[81,96]{1,0:T(8,128)}) all-reduce(f32[49,96]{1,0:T(8,128)S(1)} %copy.694, f32[96]{0:T(128)S(1)} %dynamic-slice.6, ...), channel_id=1, replica_groups=mesh['dp'=4,'fsdp'=8] {'dp'}, use_global_device_ids=true, to_apply=%region_55.56 | all-reduce | flops 13344 | bytes 106752 | tf_op jit(solution)/shard_map/psum | solution.py:213
  513.8 56.6 %all-reduce.116.cloned.1.call-done = (f32[96,3072]{1,0:T(8,128)}, f32[384,768]{1,0:T(8,128)}) async-done(((f32[96,3072]{1,0:T(8,128)}, f32[384,768]{1,0:T(8,128)}), (f32[96,3072]{1,0:T(8,128)}, f32[384,768]{1,0:T(8,128)})) %all-reduce.116.cloned.1.call-update) | async-done | bytes 2359312 | tf_op jit(solution)/shard_map/psum | solution.py:213
  570.4 2.5 copy.736
  572.9 1.0 copy.737
  (409 shorter events, 42.0 us)
Async XLA Ops:
  7.2 20.0 %copy-start.17 = (bf16[4,2,10,10,768]{4,1,3,2,0:T(2,128)(2,1)S(1)}, bf16[4,2,10,10,768]{4,1,3,2,0:T(2,128)(2,1)}, u32[]{:S(2)}) copy-start(bf16[4,2,10,10,768]{4,1,3,2,0:T(2,128)(2,1)} %param.16) | copy-start | bytes 3686404
  7.2 131.0 %all-gather.6.cloned.1.call-start = ((), (), s32[]{:S(2)}) async-start(), calls=%async_computation.4 | async-start | bytes 5308416 | tf_op jit(solution)/shard_map/all_gather | solution.py:87
  7.9 159.6 %all-gather.8.cloned.1.call-start = ((), (), s32[]{:S(2)}) async-start(), calls=%async_computation.5 | async-start | bytes 5308416 | tf_op jit(solution)/shard_map/all_gather | solution.py:89
  8.7 406.1 %reduce-scatter.9.cloned.1.call-start = ((), (), s32[]{:S(2)}) async-start(), calls=%async_computation.6 | async-start | bytes 10616832 | tf_op jit(solution)/shard_map/reduce_scatter | solution.py:194
  9.6 194.6 %copy-start.27 = (f32[4,100]{1,0:T(4,128)}, f32[4,100]{1,0:T(4,128)S(1)}, u32[]{:S(2)}) copy-start(f32[4,100]{1,0:T(4,128)S(1)} %reshape.601) | copy-start | bytes 4804
  9.8 18.0 %copy-start.24 = (f32[4,10,10]{0,2,1:T(8,128)}, f32[4,10,10]{0,2,1:T(8,128)S(1)}, u32[]{:S(2)}) copy-start(f32[4,10,10]{0,2,1:T(8,128)S(1)} %copy.561) | copy-start | bytes 4804
  26.0 43.5 %copy-start.29 = (f32[768]{0:T(1024)}, f32[768]{0:T(1024)S(1)}, u32[]{:S(2)}) copy-start(f32[768]{0:T(1024)S(1)} %get-tuple-element.161) | copy-start | bytes 9220
  26.0 43.5 %copy-start.31 = (f32[768]{0:T(1024)}, f32[768]{0:T(1024)S(1)}, u32[]{:S(2)}) copy-start(f32[768]{0:T(1024)S(1)} %get-tuple-element.162) | copy-start | bytes 9220
  26.0 43.5 %copy-start.33 = (f32[768]{0:T(1024)}, f32[768]{0:T(1024)S(1)}, u32[]{:S(2)}) copy-start(f32[768]{0:T(1024)S(1)} %get-tuple-element.163) | copy-start | bytes 9220
  26.0 43.5 %copy-start.35 = (f32[768]{0:T(1024)}, f32[768]{0:T(1024)S(1)}, u32[]{:S(2)}) copy-start(f32[768]{0:T(1024)S(1)} %get-tuple-element.164) | copy-start | bytes 9220
  26.0 43.5 %copy-start.37 = (f32[768]{0:T(1024)}, f32[768]{0:T(1024)S(1)}, u32[]{:S(2)}) copy-start(f32[768]{0:T(1024)S(1)} %get-tuple-element.165) | copy-start | bytes 9220
  26.0 43.5 %copy-start.39 = (f32[768]{0:T(1024)}, f32[768]{0:T(1024)S(1)}, u32[]{:S(2)}) copy-start(f32[768]{0:T(1024)S(1)} %get-tuple-element.166) | copy-start | bytes 9220
  26.1 43.5 %copy-start.41 = (f32[768]{0:T(1024)}, f32[768]{0:T(1024)S(1)}, u32[]{:S(2)}) copy-start(f32[768]{0:T(1024)S(1)} %get-tuple-element.167) | copy-start | bytes 9220
  26.1 43.5 %copy-start.43 = (f32[768]{0:T(1024)}, f32[768]{0:T(1024)S(1)}, u32[]{:S(2)}) copy-start(f32[768]{0:T(1024)S(1)} %get-tuple-element.168) | copy-start | bytes 9220
  26.1 43.5 %copy-start.45 = (f32[768]{0:T(1024)}, f32[768]{0:T(1024)S(1)}, u32[]{:S(2)}) copy-start(f32[768]{0:T(1024)S(1)} %get-tuple-element.169) | copy-start | bytes 9220
  26.1 43.5 %copy-start.47 = (f32[768]{0:T(1024)}, f32[768]{0:T(1024)S(1)}, u32[]{:S(2)}) copy-start(f32[768]{0:T(1024)S(1)} %get-tuple-element.170) | copy-start | bytes 9220
  26.1 43.5 %copy-start.49 = (f32[768]{0:T(1024)}, f32[768]{0:T(1024)S(1)}, u32[]{:S(2)}) copy-start(f32[768]{0:T(1024)S(1)} %get-tuple-element.171) | copy-start | bytes 9220
  26.3 43.3 %copy-start.51 = (f32[768]{0:T(1024)}, f32[768]{0:T(1024)S(1)}, u32[]{:S(2)}) copy-start(f32[768]{0:T(1024)S(1)} %get-tuple-element.142) | copy-start | bytes 9220
  26.3 43.3 %copy-start.53 = (f32[768]{0:T(1024)}, f32[768]{0:T(1024)S(1)}, u32[]{:S(2)}) copy-start(f32[768]{0:T(1024)S(1)} %get-tuple-element.157) | copy-start | bytes 9220
  26.3 43.3 %copy-start.55 = (f32[768]{0:T(1024)}, f32[768]{0:T(1024)S(1)}, u32[]{:S(2)}) copy-start(f32[768]{0:T(1024)S(1)} %get-tuple-element.158) | copy-start | bytes 9220
  26.3 43.3 %copy-start.57 = (f32[768]{0:T(1024)}, f32[768]{0:T(1024)S(1)}, u32[]{:S(2)}) copy-start(f32[768]{0:T(1024)S(1)} %get-tuple-element.159) | copy-start | bytes 9220
  26.3 43.3 %copy-start.59 = (f32[768]{0:T(1024)}, f32[768]{0:T(1024)S(1)}, u32[]{:S(2)}) copy-start(f32[768]{0:T(1024)S(1)} %get-tuple-element.160) | copy-start | bytes 9220
  26.3 43.3 %copy-start.64 = (f32[768]{0:T(1024)}, f32[768]{0:T(1024)S(1)}, u32[]{:S(2)}) copy-start(f32[768]{0:T(1024)S(1)} %get-tuple-element.143) | copy-start | bytes 9220
  26.3 43.3 %copy-start.65 = (f32[768]{0:T(1024)}, f32[768]{0:T(1024)S(1)}, u32[]{:S(2)}) copy-start(f32[768]{0:T(1024)S(1)} %get-tuple-element.144) | copy-start | bytes 9220
  26.3 43.3 %copy-start.66 = (f32[768]{0:T(1024)}, f32[768]{0:T(1024)S(1)}, u32[]{:S(2)}) copy-start(f32[768]{0:T(1024)S(1)} %get-tuple-element.145) | copy-start | bytes 9220
  26.4 43.3 %copy-start.67 = (f32[768]{0:T(1024)}, f32[768]{0:T(1024)S(1)}, u32[]{:S(2)}) copy-start(f32[768]{0:T(1024)S(1)} %get-tuple-element.146) | copy-start | bytes 9220
  26.4 43.3 %copy-start.68 = (f32[768]{0:T(1024)}, f32[768]{0:T(1024)S(1)}, u32[]{:S(2)}) copy-start(f32[768]{0:T(1024)S(1)} %get-tuple-element.147) | copy-start | bytes 9220
  26.4 43.3 %copy-start.69 = (f32[768]{0:T(1024)}, f32[768]{0:T(1024)S(1)}, u32[]{:S(2)}) copy-start(f32[768]{0:T(1024)S(1)} %get-tuple-element.148) | copy-start | bytes 9220
  26.4 43.3 %copy-start.70 = (f32[768]{0:T(1024)}, f32[768]{0:T(1024)S(1)}, u32[]{:S(2)}) copy-start(f32[768]{0:T(1024)S(1)} %get-tuple-element.149) | copy-start | bytes 9220
  26.4 43.3 %copy-start.71 = (f32[768]{0:T(1024)}, f32[768]{0:T(1024)S(1)}, u32[]{:S(2)}) copy-start(f32[768]{0:T(1024)S(1)} %get-tuple-element.150) | copy-start | bytes 9220
  26.4 43.3 %copy-start.72 = (f32[768]{0:T(1024)}, f32[768]{0:T(1024)S(1)}, u32[]{:S(2)}) copy-start(f32[768]{0:T(1024)S(1)} %get-tuple-element.151) | copy-start | bytes 9220
  26.4 43.3 %copy-start.73 = (f32[768]{0:T(1024)}, f32[768]{0:T(1024)S(1)}, u32[]{:S(2)}) copy-start(f32[768]{0:T(1024)S(1)} %get-tuple-element.152) | copy-start | bytes 9220
  26.4 43.3 %copy-start.74 = (f32[768]{0:T(1024)}, f32[768]{0:T(1024)S(1)}, u32[]{:S(2)}) copy-start(f32[768]{0:T(1024)S(1)} %get-tuple-element.153) | copy-start | bytes 9220
  26.4 43.3 %copy-start.75 = (f32[768]{0:T(1024)}, f32[768]{0:T(1024)S(1)}, u32[]{:S(2)}) copy-start(f32[768]{0:T(1024)S(1)} %get-tuple-element.154) | copy-start | bytes 9220
  26.4 43.3 %copy-start.76 = (f32[768]{0:T(1024)}, f32[768]{0:T(1024)S(1)}, u32[]{:S(2)}) copy-start(f32[768]{0:T(1024)S(1)} %get-tuple-element.155) | copy-start | bytes 9220
  26.5 43.3 %copy-start.77 = (f32[768]{0:T(1024)}, f32[768]{0:T(1024)S(1)}, u32[]{:S(2)}) copy-start(f32[768]{0:T(1024)S(1)} %get-tuple-element.156) | copy-start | bytes 9220
  27.2 42.6 %copy-start.61 = (f32[768]{0:T(1024)}, f32[768]{0:T(1024)S(1)}, u32[]{:S(2)}) copy-start(f32[768]{0:T(1024)S(1)} %get-tuple-element.123) | copy-start | bytes 9220
  27.2 42.6 %copy-start.63 = (f32[768]{0:T(1024)}, f32[768]{0:T(1024)S(1)}, u32[]{:S(2)}) copy-start(f32[768]{0:T(1024)S(1)} %get-tuple-element.124) | copy-start | bytes 9220
  27.2 42.6 %copy-start.78 = (f32[768]{0:T(1024)}, f32[768]{0:T(1024)S(1)}, u32[]{:S(2)}) copy-start(f32[768]{0:T(1024)S(1)} %get-tuple-element.125) | copy-start | bytes 9220
  27.2 42.6 %copy-start.79 = (f32[768]{0:T(1024)}, f32[768]{0:T(1024)S(1)}, u32[]{:S(2)}) copy-start(f32[768]{0:T(1024)S(1)} %get-tuple-element.139) | copy-start | bytes 9220
  27.2 42.6 %copy-start.80 = (f32[768]{0:T(1024)}, f32[768]{0:T(1024)S(1)}, u32[]{:S(2)}) copy-start(f32[768]{0:T(1024)S(1)} %get-tuple-element.140) | copy-start | bytes 9220
  27.2 42.6 %copy-start.81 = (f32[768]{0:T(1024)}, f32[768]{0:T(1024)S(1)}, u32[]{:S(2)}) copy-start(f32[768]{0:T(1024)S(1)} %get-tuple-element.141) | copy-start | bytes 9220
  69.5 18.1 %copy-start = (f32[8,10,10,768]{3,0,2,1:T(8,128)}, f32[8,10,10,768]{3,0,2,1:T(8,128)S(1)}, u32[]{:S(2)}) copy-start(f32[8,10,10,768]{3,0,2,1:T(8,128)S(1)} %reshape.592) | copy-start | bytes 7372804
  90.0 16.2 %copy-start.84 = (bf16[81,96]{1,0:T(8,128)(2,1)S(1)}, bf16[81,96]{1,0:T(8,128)(2,1)}, u32[]{:S(2)}) copy-start(bf16[81,96]{1,0:T(8,128)(2,1)} %param.31) | copy-start | bytes 46660
  90.0 30.9 %copy-start.128 = (s32[4,100,4]{1,2,0:T(4,128)S(1)}, s32[4,100,4]{1,2,0:T(4,128)}, u32[]{:S(2)}) copy-start(s32[4,100,4]{1,2,0:T(4,128)} %param.19) | copy-start | bytes 19204
  90.0 31.1 %copy-start.129 = (f32[4,100,4]{1,2,0:T(4,128)S(1)}, f32[4,100,4]{1,2,0:T(4,128)}, u32[]{:S(2)}) copy-start(f32[4,100,4]{1,2,0:T(4,128)} %param.20) | copy-start | bytes 19204
  92.9 74.6 %copy-start.89 = (f32[768]{0:T(1024)}, f32[768]{0:T(1024)S(1)}, u32[]{:S(2)}) copy-start(f32[768]{0:T(1024)S(1)} %convert_element_type.113) | copy-start | bytes 9220
  106.3 126.1 %copy-start.87 = (f32[800]{0:T(1024)}, f32[800]{0:T(1024)S(1)}, u32[]{:S(2)}) copy-start(f32[800]{0:T(1024)S(1)} %mul.1320) | copy-start | bytes 9604
  180.1 23.0 %copy-start.2 = (f32[4,2,100,768]{3,2,1,0:T(8,128)}, f32[4,2,100,768]{3,2,1,0:T(8,128)S(1)}, u32[]{:S(2)}) copy-start(f32[4,2,100,768]{3,2,1,0:T(8,128)S(1)} %reshape.594) | copy-start | bytes 7372804
  207.1 16.7 %copy-start.7 = (f32[800,768]{1,0:T(8,128)S(1)}, f32[800,768]{1,0:T(8,128)}, u32[]{:S(2)}) copy-start(f32[800,768]{1,0:T(8,128)} %copy-done.6) | copy-start | bytes 7372804
  232.3 198.1 %reduce-scatter.11.cloned.1.call-start = ((), (), s32[]{:S(2)}) async-start(), calls=%async_computation.7 | async-start | bytes 10616832 | tf_op jit(solution)/shard_map/reduce_scatter | solution.py:196
  242.6 223.7 %reduce-scatter.13.cloned.1.call-start = ((), (), s32[]{:S(2)}) async-start(), calls=%async_computation.8 | async-start | bytes 442368
  317.7 15.4 %copy-start.30 = (f32[768]{0:T(1024)S(1)}, f32[768]{0:T(1024)}, u32[]{:S(2)}) copy-start(f32[768]{0:T(1024)} %copy-done.29) | copy-start | bytes 9220
  317.7 15.4 %copy-start.32 = (f32[768]{0:T(1024)S(1)}, f32[768]{0:T(1024)}, u32[]{:S(2)}) copy-start(f32[768]{0:T(1024)} %copy-done.31) | copy-start | bytes 9220
  317.7 15.4 %copy-start.34 = (f32[768]{0:T(1024)S(1)}, f32[768]{0:T(1024)}, u32[]{:S(2)}) copy-start(f32[768]{0:T(1024)} %copy-done.33) | copy-start | bytes 9220
  317.7 15.4 %copy-start.36 = (f32[768]{0:T(1024)S(1)}, f32[768]{0:T(1024)}, u32[]{:S(2)}) copy-start(f32[768]{0:T(1024)} %copy-done.35) | copy-start | bytes 9220
  317.7 15.4 %copy-start.38 = (f32[768]{0:T(1024)S(1)}, f32[768]{0:T(1024)}, u32[]{:S(2)}) copy-start(f32[768]{0:T(1024)} %copy-done.37) | copy-start | bytes 9220
  348.6 45.1 %copy-start.14 = (f32[8,10,10,768]{3,0,2,1:T(8,128)S(1)}, f32[8,10,10,768]{3,0,2,1:T(8,128)}, u32[]{:S(2)}) copy-start(f32[8,10,10,768]{3,0,2,1:T(8,128)} %get-tuple-element.207) | copy-start | bytes 7372804
  348.7 45.1 %copy-start.15 = (f32[8,10,10,768]{3,0,2,1:T(8,128)S(1)}, f32[8,10,10,768]{3,0,2,1:T(8,128)}, u32[]{:S(2)}) copy-start(f32[8,10,10,768]{3,0,2,1:T(8,128)} %get-tuple-element.208) | copy-start | bytes 7372804
  411.8 81.9 %reduce-scatter.15.cloned.1.call-start = ((), (), s32[]{:S(2)}) async-start(), calls=%async_computation.9 | async-start | bytes 442368
  411.9 19.9 %copy-start.3 = (f32[4,2,100,768]{3,2,1,0:T(8,128)S(1)}, f32[4,2,100,768]{3,2,1,0:T(8,128)}, u32[]{:S(2)}) copy-start(f32[4,2,100,768]{3,2,1,0:T(8,128)} %copy-done.2) | copy-start | bytes 7372804
  411.9 19.9 %copy-start.22 = (bf16[768,81,1]{0,1,2:T(8,128)(2,1)S(1)}, bf16[768,81,1]{0,1,2:T(8,128)(2,1)}, u32[]{:S(2)}) copy-start(bf16[768,81,1]{0,1,2:T(8,128)(2,1)} %copy-done.21) | copy-start | bytes 373252
  414.7 155.7 %all-reduce.116.cloned.1.call-start = ((), (), s32[]{:S(2)}) async-start(), calls=%async_computation.10 | async-start | bytes 4718592 | tf_op jit(solution)/shard_map/psum | solution.py:213
  435.6 27.3 %copy-start.13 = (f32[4,2,10,10,768]{4,0,3,2,1:T(4,128)S(1)}, f32[4,2,10,10,768]{4,0,3,2,1:T(4,128)}, u32[]{:S(2)}) copy-start(f32[4,2,10,10,768]{4,0,3,2,1:T(4,128)} %get-tuple-element.258) | copy-start | bytes 7372804
  (83 other events, 649.2 us)
Sparse Core Ops, SparseCore 0:
  9.7 55.0 all-gather.5
  66.4 51.5 all-gather.7
  232.4 97.8 reduce-scatter.8
  332.5 97.8 reduce-scatter.10
  433.1 28.9 reduce-scatter.12
  464.9 28.8 reduce-scatter.14
  496.9 73.5 all-reduce.115
where the time goes:
time: 591 us; the launch traced here: 581 us
  other arithmetic  142 us (24%)
  blocking collectives  119 us (20%)
  matrix products  104 us (18%)
  waiting for transfers between devices  100 us (17%)
  local copies, waits for them, and re-layouts  97.1 us (16%)
  between operations  18.8 us (3%)
    psum x1, waiting for transfers between devices, shards(): lax.psum((part_kernel, part_cbias, part_gain, part_shift, part_win, part_...  56.6 us
    unnamed x2, blocking collectives  56.4 us
    add_any x2, other arithmetic, depthwise(): padded[:, row_tap:row_tap + CANVAS, col_tap:col_tap + CANVAS, :]  49 us
    mul x3, other arithmetic, depthwise(): padded[:, row_tap:row_tap + CANVAS, col_tap:col_tap + CANVAS, :]  39.8 us
    dot_general x1, matrix products, shards(): jnp.dot(normed_low, win_all, preferred_element_type=jnp.float32)  29.2 us
    broadcast_in_dim x49, local copies, waits for them, and re-layouts, depthwise(): kernel[row_tap * KERNEL + col_tap]  28.3 us
    unnamed x9, waiting for transfers between devices  28 us
    reduce_sum x4, other arithmetic, depthwise(): padded[:, row_tap:row_tap + CANVAS, col_tap:col_tap + CANVAS, :]  22.8 us
  transfers between devices with their start and end apart: 7, of which 3 were waited for; matrix products, arithmetic and copies ran while one was open for 47% of the time, Pallas kernels for 0%

commit v1 on v0

v1 whole, which is shorter than its diff:
```python
import functools

import jax
import jax.numpy as jnp
import numpy as np
from jax import lax
from jax.experimental import pallas as pl
from jax.experimental.pallas import tpu as pltpu
from jax.sharding import PartitionSpec as P

CANVAS = 10
KERNEL = 7
REACH = KERNEL // 2
TAPS = KERNEL * KERNEL
WINDOW = 9
PIX = CANVAS * CANVAS
PADDED = 104
LANES = 128
EPSILON = 1e-06
f32 = jnp.float32
bf16 = jnp.bfloat16
VMEM_LIMIT = 56 * 1024 * 1024


def params(limit=VMEM_LIMIT):
    return pltpu.CompilerParams(vmem_limit_bytes=limit)


def cost(flops, nbytes, trans=0):
    return pl.CostEstimate(flops=int(flops), bytes_accessed=int(nbytes), transcendentals=int(trans))


def whole(shape):
    return pl.BlockSpec(shape, lambda *_: (0,) * len(shape))


def conv_rows(src, kernel_ref, cols, flip, finish):
    for row in range(CANVAS):
        sums = [None] * CANVAS
        for ky in range(KERNEL):
            source_row = row + ky - REACH
            if not 0 <= source_row < CANVAS:
                continue
            cells = [src[source_row * CANVAS + col, :, cols] for col in range(CANVAS)]
            for kx in range(KERNEL):
                tap = ky * KERNEL + kx
                tap = TAPS - 1 - tap if flip else tap
                weight = jnp.broadcast_to(kernel_ref[pl.ds(tap, 1), cols], cells[0].shape)
                for col in range(CANVAS):
                    source = col + kx - REACH
                    if 0 <= source < CANVAS:
                        term = cells[source] * weight
                        sums[col] = term if sums[col] is None else sums[col] + term
        for col in range(CANVAS):
            finish(row * CANVAS + col, sums[col])


def conv_norm_kernel(x_ref, kernel_ref, cbias_ref, gain_ref, shift_ref, normed_ref, xhat_ref, rstd_ref, xf, cf):
    frames = xf.shape[1]
    channels = xf.shape[2]
    xf[...] = x_ref[...].astype(f32).reshape(xf.shape)

    @pl.loop(0, channels // LANES)
    def _(tile):
        cols = pl.ds(pl.multiple_of(tile * LANES, LANES), LANES)

        def finish(cell, total):
            cf[cell, :, cols] = total + jnp.broadcast_to(cbias_ref[:, cols], total.shape)

        conv_rows(xf, kernel_ref, cols, False, finish)

    step = 10

    @pl.loop(0, PIX // step)
    def _(block):
        values = cf[pl.ds(block * step, step)].reshape(step * frames, channels)
        mean = jnp.sum(values, axis=-1, keepdims=True) * (1.0 / channels)
        centred = values - mean
        variance = jnp.sum(centred * centred, axis=-1, keepdims=True) * (1.0 / channels)
        scale = lax.rsqrt(variance + EPSILON)
        xhat = centred * scale
        rows = pl.ds(pl.multiple_of(block * step * frames, step * frames), step * frames)
        xhat_ref[rows, :] = xhat
        rstd_ref[rows, :] = scale
        normed_ref[rows, :] = (xhat * gain_ref[...] + shift_ref[...]).astype(bf16)


def conv_norm(x_rows, kernel, cbias, gain, shift, frames):
    rows, channels = x_rows.shape
    shape = (PIX, frames, channels)
    return pl.pallas_call(
        conv_norm_kernel,
        name="conv_norm",
        out_shape=(
            jax.ShapeDtypeStruct((rows, channels), bf16),
            jax.ShapeDtypeStruct((rows, channels), f32),
            jax.ShapeDtypeStruct((rows, 1), f32),
        ),
        scratch_shapes=[pltpu.VMEM(shape, f32), pltpu.VMEM(shape, f32)],
        compiler_params=params(),
        cost_estimate=cost(2 * TAPS * rows * channels * 20, rows * channels * 8),
    )(x_rows, kernel, cbias, gain, shift)


def gelu_pair(hidden):
    cdf = 0.5 * lax.erf(hidden * 0.7071067811865476) + 0.5
    density = jnp.exp(hidden * hidden * -0.5) * 0.3989422804014327
    return hidden * cdf, cdf + hidden * density


def widen_kernel(chunks, normed_ref, weight_ref, bias_ref, active_ref, slope_ref):
    size = normed_ref.shape[0] // chunks
    for chunk in range(chunks):
        rows = pl.ds(chunk * size, size)
        hidden = jnp.dot(normed_ref[rows, :], weight_ref[...], preferred_element_type=f32) + bias_ref[...]
        active, slope = gelu_pair(hidden)
        active_ref[rows, :] = active.astype(bf16)
        slope_ref[rows, :] = slope.astype(bf16)


def widen(normed, weight, bias, tile=384, chunks=5):
    rows, channels = normed.shape
    units = weight.shape[1]
    block = pl.BlockSpec((rows, tile), lambda i: (0, i))
    return pl.pallas_call(
        functools.partial(widen_kernel, chunks),
        name="widen",
        grid=(units // tile,),
        in_specs=[
            whole((rows, channels)),
            pl.BlockSpec((channels, tile), lambda i: (0, i)),
            pl.BlockSpec((1, tile), lambda i: (0, i)),
        ],
        out_specs=(block, block),
        out_shape=(jax.ShapeDtypeStruct((rows, units), bf16),) * 2,
        compiler_params=params(),
        cost_estimate=cost(2 * rows * channels * units * 2, 2 * (rows * channels + channels * units + 2 * rows * units)),
    )(normed, weight, bias)


def narrow_kernel(active_ref, weight_ref, bias_ref, branch_ref):
    part = jnp.dot(active_ref[...], weight_ref[...], preferred_element_type=f32)

    @pl.when(pl.program_id(0) == 0)
    def _():
        branch_ref[...] = part + bias_ref[...]

    @pl.when(pl.program_id(0) > 0)
    def _():
        branch_ref[...] += part


def narrow(active, weight, bias, tile=512):
    rows, units = active.shape
    channels = weight.shape[1]
    return pl.pallas_call(
        narrow_kernel,
        name="narrow",
        grid=(units // tile,),
        in_specs=[
            pl.BlockSpec((rows, tile), lambda i: (0, i)),
            pl.BlockSpec((tile, channels), lambda i: (i, 0)),
            whole((1, channels)),
        ],
        out_specs=whole((rows, channels)),
        out_shape=jax.ShapeDtypeStruct((rows, channels), f32),
        compiler_params=params(),
        cost_estimate=cost(2 * rows * channels * units, 2 * (rows * units + channels * units + 2 * rows * channels)),
    )(active, weight, bias)


def skew(values, inverse):
    rows = lax.broadcasted_iota(jnp.int32, values.shape, 0)
    centre = (WINDOW // 2) * (CANVAS + 1)
    amount = centre - rows if not inverse else rows - centre
    amount = jnp.bitwise_and(amount, LANES - 1)
    for bit in range(7):
        moved = pltpu.roll(values, 1 << bit, 1)
        values = jnp.where(jnp.bitwise_and(amount, 1 << bit) != 0, moved, values)
    return values


def split(values):
    high = values.astype(bf16)
    return high, (values - high.astype(f32)).astype(bf16)


def nt(left, right):
    return lax.dot_general(left, right, (((1,), (1,)), ((), ())), preferred_element_type=f32)


def tn(left, right):
    return lax.dot_general(left, right, (((0,), (0,)), ((), ())), preferred_element_type=f32)


def flow_kernel(
    images,
    x_ref,
    branch_ref,
    scale_ref,
    mask_ref,
    cell_mask_ref,
    upstream_ref,
    index_ref,
    weight_ref,
    place_ref,
    west_ref,
    window_ref,
    out_ref,
    dmixed_ref,
    dbranch_ref,
    gscale_ref,
    gbout_ref,
    gwest_ref,
    mixed,
    back,
):
    rows, channels = branch_ref.shape
    frames = 2 * images
    factor = channels ** (-0.5)
    tiles = channels // LANES
    for tile in range(tiles):
        cols = pl.ds(tile * LANES, LANES)
        total = x_ref[:, cols].astype(f32) + scale_ref[:, cols] * branch_ref[:, cols]
        mixed[tile, pl.ds(0, rows), :] = total * mask_ref[...]
        mixed[tile, pl.ds(rows, PADDED * frames - rows), :] = jnp.zeros((PADDED * frames - rows, LANES), f32)

    def take(frame):
        rows_of = pl.ds(frame, PADDED, stride=frames)
        return jnp.concatenate([mixed[tile, rows_of, :] for tile in range(tiles)], axis=1)

    def put(frame, values):
        rows_of = pl.ds(frame, PADDED, stride=frames)
        for tile in range(tiles):
            back[tile, rows_of, :] = values[:, tile * LANES : (tile + 1) * LANES]

    lanes = lax.broadcasted_iota(jnp.int32, (LANES, LANES), 0)
    chosen = (lanes == place_ref[...]).astype(bf16)
    west = jnp.dot(chosen, west_ref[...], preferred_element_type=f32).astype(bf16)
    window = window_ref[...]
    cells = lax.broadcasted_iota(jnp.int32, (PADDED, LANES), 1)
    gwest = jnp.zeros((LANES, channels), f32)
    for image in range(images):
        first = take(image)
        second = take(images + image)
        inside = cell_mask_ref[image]
        first_low = first.astype(bf16)
        second_low = second.astype(bf16)
        warp = jnp.zeros((PADDED, LANES), f32)
        for corner in range(4):
            place = index_ref[image, :, pl.ds(corner, 1)]
            amount = weight_ref[image, :, pl.ds(corner, 1)]
            warp = warp + jnp.where(cells == place, amount, 0.0)
        warp_high, warp_low = split(warp[:, :PADDED])
        warped = (
            jnp.dot(warp_high, second_low, preferred_element_type=f32)
            + jnp.dot(warp_low, second_low, preferred_element_type=f32)
        ).astype(bf16)
        warped_wide = jnp.concatenate([warped, jnp.zeros((LANES - PADDED, channels), bf16)], axis=0)
        scores = nt(first_low, warped_wide)
        costs = skew(scores, False) * window * factor
        gated, slope = gelu_pair(costs)
        gated_low = gated.astype(bf16)
        head = jnp.dot(gated_low, west, preferred_element_type=f32)
        out_ref[image, 0] = ((first + head) * inside)[:PIX].astype(bf16)
        out_ref[image, 1] = second_low[:PIX]
        d_first = upstream_ref[image, 0].astype(f32) * inside
        d_head = d_first.astype(bf16)
        gwest = gwest + tn(gated_low, d_head)
        d_costs = slope * nt(d_head, west) * window * factor
        d_scores = skew(d_costs, True).astype(bf16)
        d_first = d_first + jnp.dot(d_scores, warped_wide, preferred_element_type=f32)
        d_warped = tn(d_scores, first_low)[:PADDED].astype(bf16)
        d_second = upstream_ref[image, 1].astype(f32) + tn(warp_high, d_warped) + tn(warp_low, d_warped)
        put(image, d_first)
        put(images + image, d_second)
    gwest_ref[...] = gwest
    for tile in range(tiles):
        cols = pl.ds(tile * LANES, LANES)
        d_mixed = back[tile, pl.ds(0, rows), :] * mask_ref[...]
        dmixed_ref[:, cols] = d_mixed
        gscale_ref[:, cols] = jnp.sum(d_mixed * branch_ref[:, cols], axis=0, keepdims=True)
        d_branch = (d_mixed * scale_ref[:, cols]).astype(bf16)
        dbranch_ref[:, cols] = d_branch
        gbout_ref[:, cols] = jnp.sum(d_branch.astype(f32), axis=0, keepdims=True)


def window_table():
    cells = np.arange(PADDED)[:, None]
    lane = np.arange(LANES)[None, :]
    reach = WINDOW // 2
    row = cells // CANVAS + lane // CANVAS - reach
    col = cells % CANVAS + lane % CANVAS - reach
    good = (lane % CANVAS < WINDOW) & (lane // CANVAS < WINDOW) & (cells < PIX)
    good &= (row >= 0) & (row < CANVAS) & (col >= 0) & (col < CANVAS)
    return good.astype(np.float32)


def flow(x_rows, branch, scale, mask, cell_mask, upstream, index, weight, place, west):
    rows, channels = branch.shape
    images = upstream.shape[0]
    frames = 2 * images
    window = jnp.asarray(window_table())
    return pl.pallas_call(
        functools.partial(flow_kernel, images),
        name="flow",
        out_shape=(
            jax.ShapeDtypeStruct((images, 2, PIX, channels), bf16),
            jax.ShapeDtypeStruct((rows, channels), f32),
            jax.ShapeDtypeStruct((rows, channels), bf16),
            jax.ShapeDtypeStruct((1, channels), f32),
            jax.ShapeDtypeStruct((1, channels), f32),
            jax.ShapeDtypeStruct((LANES, channels), f32),
        ),
        scratch_shapes=[
            pltpu.VMEM((channels // LANES, PADDED * frames, LANES), f32),
            pltpu.VMEM((channels // LANES, PADDED * frames, LANES), f32),
        ],
        compiler_params=params(),
        cost_estimate=cost(4e9, rows * channels * 16),
    )(x_rows, branch, scale, mask, cell_mask, upstream, index, weight, place, west, window)


def grad_narrow_kernel(dbranch_t_ref, active_ref, out_ref):
    out_ref[0] = jnp.dot(dbranch_t_ref[...], active_ref[...], preferred_element_type=f32).astype(bf16)


def grad_narrow(dbranch_t, active, blocks=8):
    channels, rows = dbranch_t.shape
    units = active.shape[1]
    tile = units // blocks
    return pl.pallas_call(
        grad_narrow_kernel,
        name="grad_narrow",
        grid=(blocks,),
        in_specs=[whole((channels, rows)), pl.BlockSpec((rows, tile), lambda i: (0, i))],
        out_specs=pl.BlockSpec((1, channels, tile), lambda i: (i, 0, 0)),
        out_shape=jax.ShapeDtypeStruct((blocks, channels, tile), bf16),
        compiler_params=params(),
        cost_estimate=cost(2 * rows * channels * units, 2 * (rows * units + channels * units + rows * channels)),
    )(dbranch_t, active)


def hidden_back_kernel(dbranch_ref, weight_ref, slope_ref, normed_t_ref, dhidden_ref, gbin_ref, gwin_ref):
    d_active = nt(dbranch_ref[...], weight_ref[...])
    d_hidden = (d_active * slope_ref[...].astype(f32)).astype(bf16)
    dhidden_ref[...] = d_hidden
    gbin_ref[...] = jnp.sum(d_hidden.astype(f32), axis=0, keepdims=True)
    gwin_ref[0] = jnp.dot(normed_t_ref[...], d_hidden, preferred_element_type=f32).astype(bf16)


def hidden_back(dbranch, weight, slope, normed_t, blocks=8):
    rows, channels = dbranch.shape
    units = weight.shape[0]
    tile = units // blocks
    return pl.pallas_call(
        hidden_back_kernel,
        name="hidden_back",
        grid=(blocks,),
        in_specs=[
            whole((rows, channels)),
            pl.BlockSpec((tile, channels), lambda i: (i, 0)),
            pl.BlockSpec((rows, tile), lambda i: (0, i)),
            whole((channels, rows)),
        ],
        out_specs=(
            pl.BlockSpec((rows, tile), lambda i: (0, i)),
            pl.BlockSpec((1, tile), lambda i: (0, i)),
            pl.BlockSpec((1, channels, tile), lambda i: (i, 0, 0)),
        ),
        out_shape=(
            jax.ShapeDtypeStruct((rows, units), bf16),
            jax.ShapeDtypeStruct((1, units), f32),
            jax.ShapeDtypeStruct((blocks, channels, tile), bf16),
        ),
        compiler_params=params(),
        cost_estimate=cost(4 * rows * channels * units, 2 * (3 * rows * units + 2 * channels * units)),
    )(dbranch, weight, slope, normed_t)


def norm_back_kernel(dhidden_ref, weight_ref, xhat_ref, rstd_ref, gain_ref, dconv_ref, ggain_ref, gshift_ref, gcbias_ref):
    step = pl.program_id(0)
    part = nt(dhidden_ref[...], weight_ref[...])

    @pl.when(step == 0)
    def _():
        dconv_ref[...] = part

    @pl.when(step > 0)
    def _():
        dconv_ref[...] += part

    @pl.when(step == pl.num_programs(0) - 1)
    def _():
        rows, channels = dconv_ref.shape
        size = 80
        ggain_ref[...] = jnp.zeros_like(ggain_ref)
        gshift_ref[...] = jnp.zeros_like(gshift_ref)
        gcbias_ref[...] = jnp.zeros_like(gcbias_ref)

        @pl.loop(0, rows // size)
        def _(block):
            span = pl.ds(pl.multiple_of(block * size, size), size)
            d_normed = dconv_ref[span, :]
            xhat = xhat_ref[span, :]
            product = d_normed * xhat
            ggain_ref[...] += jnp.sum(product, axis=0, keepdims=True)
            gshift_ref[...] += jnp.sum(d_normed, axis=0, keepdims=True)
            d_xhat = d_normed * gain_ref[...]
            mean = jnp.sum(d_xhat, axis=-1, keepdims=True) * (1.0 / channels)
            along = jnp.sum(product * gain_ref[...], axis=-1, keepdims=True) * (1.0 / channels)
            d_conv = (d_xhat - mean - xhat * along) * rstd_ref[span, :]
            dconv_ref[span, :] = d_conv
            gcbias_ref[...] += jnp.sum(d_conv, axis=0, keepdims=True)


def norm_back(dhidden, weight, xhat, rstd, gain, tile=768):
    rows, units = dhidden.shape
    channels = weight.shape[0]
    vector = jax.ShapeDtypeStruct((1, channels), f32)
    return pl.pallas_call(
        norm_back_kernel,
        name="norm_back",
        grid=(units // tile,),
        in_specs=[
            pl.BlockSpec((rows, tile), lambda i: (0, i)),
            pl.BlockSpec((channels, tile), lambda i: (0, i)),
            whole((rows, channels)),
            whole((rows, 1)),
            whole((1, channels)),
        ],
        out_specs=(whole((rows, channels)),) + (whole((1, channels)),) * 3,
        out_shape=(jax.ShapeDtypeStruct((rows, channels), f32), vector, vector, vector),
        compiler_params=params(),
        cost_estimate=cost(2 * rows * channels * units, 2 * (rows * units + channels * units + 4 * rows * channels)),
    )(dhidden, weight, xhat, rstd, gain)


def grad_taps_kernel(x_ref, dconv_ref, out_ref, xf):
    xf[...] = x_ref[...].astype(f32).reshape(xf.shape)
    channels = xf.shape[2]

    @pl.loop(0, channels // LANES)
    def _(tile):
        cols = pl.ds(pl.multiple_of(tile * LANES, LANES), LANES)
        for ky in range(KERNEL):
            totals = [None] * KERNEL
            for row in range(CANVAS):
                source_row = row + ky - REACH
                if not 0 <= source_row < CANVAS:
                    continue
                cells = [xf[source_row * CANVAS + col, :, cols] for col in range(CANVAS)]
                grads = [dconv_ref[row * CANVAS + col, :, cols] for col in range(CANVAS)]
                for kx in range(KERNEL):
                    for col in range(CANVAS):
                        source = col + kx - REACH
                        if 0 <= source < CANVAS:
                            term = cells[source] * grads[col]
                            totals[kx] = term if totals[kx] is None else totals[kx] + term
            for kx in range(KERNEL):
                out_ref[pl.ds(ky * KERNEL + kx, 1), cols] = jnp.sum(totals[kx], axis=0, keepdims=True)


def grad_taps(x_rows, dconv, frames):
    rows, channels = x_rows.shape
    return pl.pallas_call(
        grad_taps_kernel,
        name="grad_taps",
        out_shape=jax.ShapeDtypeStruct((TAPS, channels), f32),
        scratch_shapes=[pltpu.VMEM((PIX, frames, channels), f32)],
        compiler_params=params(),
        cost_estimate=cost(2 * TAPS * rows * channels * 20, rows * channels * 6),
    )(x_rows, dconv.reshape(PIX, frames, channels))


def conv_back_kernel(dconv_ref, kernel_ref, dmixed_ref, mask_ref, out_ref):
    channels = dconv_ref.shape[2]

    @pl.loop(0, channels // LANES)
    def _(tile):
        cols = pl.ds(pl.multiple_of(tile * LANES, LANES), LANES)

        def finish(cell, total):
            out_ref[cell, :, cols] = (total + dmixed_ref[cell, :, cols]) * mask_ref[cell]

        conv_rows(dconv_ref, kernel_ref, cols, True, finish)


def conv_back(dconv, kernel, dmixed, mask, frames):
    rows, channels = dconv.shape
    shape = (PIX, frames, channels)
    return pl.pallas_call(
        conv_back_kernel,
        name="conv_back",
        out_shape=jax.ShapeDtypeStruct(shape, f32),
        compiler_params=params(),
        cost_estimate=cost(2 * TAPS * rows * channels * 20, rows * channels * 12),
    )(dconv.reshape(shape), kernel, dmixed.reshape(shape), mask.reshape(PIX, frames, 1))


def shards(
    features,
    cotangent,
    image_sizes,
    warp_index,
    warp_weight,
    offsets,
    conv_kernel,
    conv_bias,
    norm_gain,
    norm_bias,
    w_in,
    bias_in,
    w_out,
    bias_out,
    layer_scale,
    w_estimate,
):
    images = features.shape[0]
    frames = 2 * images
    channels = features.shape[-1]
    units = w_in.shape[1]

    def gather(value, axis=0):
        return lax.all_gather(value, "fsdp", axis=axis, tiled=True)

    vectors = jnp.concatenate(
        [conv_kernel, w_estimate, conv_bias[None], norm_gain[None], norm_bias[None], bias_out[None], layer_scale[None]]
    )
    vectors = gather(vectors, 1)
    kernel_all = vectors[:TAPS].astype(f32)
    west_all = vectors[TAPS : TAPS + offsets.shape[0]]
    rest = vectors[TAPS + offsets.shape[0] :].astype(f32)
    cbias_all, gain_all, shift_all, bout_all, scale_all = (rest[i : i + 1] for i in range(5))
    bin_all = gather(bias_in).astype(f32)[None]
    win_all = gather(w_in)
    wout_all = gather(w_out)

    places = jnp.arange(CANVAS, dtype=jnp.int32)
    inside = places[None, :] < image_sizes[:, None]
    side_mask = (inside[:, :, None] & inside[:, None, :]).astype(f32)
    cell_mask = jnp.pad(side_mask.reshape(images, PIX, 1), ((0, 0), (0, PADDED - PIX), (0, 0)))
    mask_rows = jnp.broadcast_to(side_mask.reshape(images, PIX).T[:, None, :], (PIX, 2, images)).reshape(-1, 1)
    masked = jnp.where(side_mask[:, None, :, :, None] != 0, features, jnp.zeros((), bf16))
    x_rows = masked.transpose(2, 3, 1, 0, 4).reshape(-1, channels)
    upstream = jnp.pad(cotangent.reshape(images, 2, PIX, channels), ((0, 0), (0, 0), (0, PADDED - PIX), (0, 0)))
    index = jnp.pad(warp_index, ((0, 0), (0, PADDED - PIX), (0, 0)))
    weight = jnp.pad(warp_weight, ((0, 0), (0, PADDED - PIX), (0, 0)))
    reach = WINDOW // 2
    lane_of = (offsets[:, 0] + reach) * CANVAS + offsets[:, 1] + reach
    count = offsets.shape[0]
    place = jnp.pad(lane_of, (0, LANES - count), constant_values=-1)[None]
    west_wide = jnp.pad(west_all, ((0, LANES - count), (0, 0)))

    normed, xhat, rstd = conv_norm(x_rows, kernel_all, cbias_all, gain_all, shift_all, frames)
    normed_t = normed.T
    active, slope = widen(normed, win_all, bin_all)
    branch = narrow(active, wout_all, bout_all)
    mixed_out, d_mixed, d_branch, g_scale, g_bout, g_west = flow(
        x_rows, branch, scale_all, mask_rows, cell_mask, upstream, index, weight, place, west_wide
    )
    g_wout = grad_narrow(d_branch.T, active)
    d_hidden, g_bin, g_win = hidden_back(d_branch, wout_all, slope, normed_t)
    d_conv, g_gain, g_shift, g_cbias = norm_back(d_hidden, win_all, xhat, rstd, gain_all)
    g_taps = grad_taps(x_rows, d_conv, frames)
    grad_rows = conv_back(d_conv, kernel_all, d_mixed, mask_rows, frames)
    grad_features = grad_rows.reshape(CANVAS, CANVAS, 2, images, channels).transpose(3, 2, 0, 1, 4)

    def reduce(value, axis):
        return lax.psum(lax.psum_scatter(value, "fsdp", scatter_dimension=axis, tiled=True).astype(f32), "dp")

    g_wout = reduce(g_wout.transpose(0, 2, 1).reshape(units, channels), 0)
    g_win = reduce(g_win.transpose(1, 0, 2).reshape(channels, units), 0)
    small = reduce(jnp.concatenate([g_taps, g_cbias, g_gain, g_shift, g_bout, g_scale, g_west]), 1)
    g_bin = reduce(g_bin[0], 0)
    return (
        mixed_out.reshape(features.shape),
        grad_features,
        small[:TAPS],
        small[TAPS],
        small[TAPS + 1],
        small[TAPS + 2],
        g_win,
        g_bin,
        g_wout,
        small[TAPS + 3],
        small[TAPS + 4],
        jnp.take(small[TAPS + 5 :], lane_of, axis=0),
    )


def solution(mesh):
    in_specs = (
        P(("dp", "fsdp"), None, None, None, None),
        P(("dp", "fsdp"), None, None, None, None),
        P(("dp", "fsdp")),
        P(("dp", "fsdp"), None, None),
        P(("dp", "fsdp"), None, None),
        P(),
        P(None, "fsdp"),
        P("fsdp"),
        P("fsdp"),
        P("fsdp"),
        P("fsdp", None),
        P("fsdp"),
        P("fsdp", None),
        P("fsdp"),
        P("fsdp"),
        P(None, "fsdp"),
    )
    out_specs = (
        P(("dp", "fsdp"), None, None, None, None),
        P(("dp", "fsdp"), None, None, None, None),
        P(None, "fsdp"),
        P("fsdp"),
        P("fsdp"),
        P("fsdp"),
        P("fsdp", None),
        P("fsdp"),
        P("fsdp", None),
        P("fsdp"),
        P("fsdp"),
        P(None, "fsdp"),
    )
    return jax.shard_map(shards, mesh=mesh, in_specs=in_specs, out_specs=out_specs, check_vma=False)
```

time: 591 us -> 477 us (0.81); the launches traced: 581 us -> 474 us
  other arithmetic: 142 us -> 4.85 us
  Pallas kernels: 0 us -> 110 us
  matrix products: 104 us -> 0 us
  local copies, waits for them, and re-layouts: 97.1 us -> 54.5 us
  waiting for transfers between devices: 100 us -> 136 us
  blocking collectives: 119 us -> 152 us
    pallas_call x0 -> x9, Pallas kernels: none -> 110 us  [the longest x1 16.9 us: hidden_back(): pl.pallas_call(hidden_back_kernel, name='hidden_back', grid=(blocks,), in...]
    dot_general x16 -> x0, matrix products: 104 us -> none  [the longest x1 29.2 us: shards(): jnp.dot(normed_low, win_all, preferred_element_type=jnp.float32)]
    psum x1, blocking collectives: 19.2 us -> 94.6 us  [reduce(): lax.psum(lax.psum_scatter(value, 'fsdp', scatter_dimension=axis, tiled=Tr...]
    psum x1, waiting for transfers between devices: 56.6 us -> 0.01 us  [reduce(): lax.psum(lax.psum_scatter(value, 'fsdp', scatter_dimension=axis, tiled=Tr...]
    add_any x4 -> x0, other arithmetic: 52.6 us -> none  [the longest x2 49 us: depthwise(): padded[:, row_tap:row_tap + CANVAS, col_tap:col_tap + CANVAS, :]]
    reduce_sum x11 -> x0, other arithmetic: 47.1 us -> none  [the longest x4 22.8 us: depthwise(): padded[:, row_tap:row_tap + CANVAS, col_tap:col_tap + CANVAS, :]]
    mul x4 -> x0, other arithmetic: 40.3 us -> none  [the longest x3 39.8 us: depthwise(): padded[:, row_tap:row_tap + CANVAS, col_tap:col_tap + CANVAS, :]]
    all_gather x2, waiting for transfers between devices: 0.04 us -> 38.9 us  [gather(): return lax.all_gather(value, 'fsdp', axis=axis, tiled=True)]
  transfers between devices with their start and end apart: 7 -> 6, of which waited for: 3 -> 4; matrix products, arithmetic and copies ran while one was open for 47% -> 11% of each run, Pallas kernels for 0% -> 10%
where the time goes in v1:
time: 477 us; the launch traced here: 474 us
  blocking collectives  152 us (32%)
  waiting for transfers between devices  136 us (29%)
  Pallas kernels  110 us (23%)
  local copies, waits for them, and re-layouts  54.5 us (11%)
  between operations  15.2 us (3%)
  other arithmetic  4.85 us (1%)
    psum x1, blocking collectives, reduce(): lax.psum(lax.psum_scatter(value, 'fsdp', scatter_dimension=axis, tiled=Tr...  94.6 us
    reduce_scatter x1, waiting for transfers between devices, reduce(): lax.psum_scatter(value, 'fsdp', scatter_dimension=axis, tiled=True)  54.1 us
    unnamed x8, waiting for transfers between devices  43.4 us
    all_gather x2, waiting for transfers between devices, gather(): return lax.all_gather(value, 'fsdp', axis=axis, tiled=True)  38.9 us
    all_gather x2, blocking collectives, gather(): return lax.all_gather(value, 'fsdp', axis=axis, tiled=True)  29.8 us
    unnamed x1, blocking collectives  28 us
    pallas_call x1, Pallas kernels, hidden_back(): pl.pallas_call(hidden_back_kernel, name='hidden_back', grid=(blocks,), in...  16.9 us
    unnamed x58, local copies, waits for them, and re-layouts  15.4 us
  transfers between devices with their start and end apart: 6, of which 4 were waited for; matrix products, arithmetic and copies ran while one was open for 11% of the time, Pallas kernels for 10%

profile of v1, /device:TPU:0, one launch (start us, length us, event | category | flops | bytes accessed | tf_op | source)
XLA Modules:
  0.0 473.8 jit_solution(6280644427965085772)
XLA Ops:
  7.2 0.7 all-gather.5.cloned.1.call-update
  8.0 0.7 all-gather.7.cloned.1.call-update
  8.7 0.7 iota_compare_fusion
  9.4 0.1 broadcast_and_fusion
  9.5 1.3 fusion
  10.9 0.5 copy.55
  11.5 1.2 reshape.138.x_ref
  12.7 0.3 concatenate.6
  13.0 16.8 %all-gather = bf16[8,96,135]{1,2,0:T(8,128)(2,1)S(1)} all-gather(bf16[1,96,135]{1,2,0:T(8,128)(2,1)S(1)} %bitcast.69), channel_id=1, replica_groups=mesh['dp'=4,'fsdp'=8] {'fsdp'}, dimensions={0}, use_global_device_ids=true | all-gather | bytes 233280 | tf_op jit(solution)/shard_map/all_gather | solution.py:525
  29.8 0.3 reshape.158
  30.1 13.1 %all-gather.1 = bf16[8,1,384]{2,1,0:T(2,128)(2,1)S(1)} all-gather(bf16[1,1,384]{2,1,0:T(2,128)(2,1)S(1)} %reshape.159), channel_id=1, replica_groups=mesh['dp'=4,'fsdp'=8] {'fsdp'}, dimensions={0}, use_global_device_ids=true | all-gather | bytes 6912 | tf_op jit(solution)/shard_map/all_gather | solution.py:525
  43.2 0.6 convert.6.bias_ref
  43.8 0.1 reshape.148
  43.9 0.1 copy.75
  44.0 1.0 reshape.168.mask_ref
  45.0 0.1 convert_element_type.49
  45.2 0.1 copy.59
  45.3 0.4 copy-done.8
  45.7 0.1 copy.60
  45.8 0.2 copy.61
  46.0 1.1 pad.28.upstream_ref
  47.2 0.7 pad.32.west_ref
  47.9 0.6 fusion.3
  48.5 0.7 slice_convert_fusion.kernel_ref
  49.2 12.3 %conv_norm.1 = (bf16[800,768]{1,0:T(8,128)(2,1)}, f32[800,768]{1,0:T(8,128)}, f32[800,1]{1,0:T(8,128)}) custom-call(bf16[800,768]{1,0:T(8,128)(2,1)} %reshape.138.x_ref, f32[49,768]{1,0:T(8,128)} %slice_convert_fusion.kernel_ref, f32[1,768]{1,0:T(1,128)} %get-tuple-element.98.cbias_ref, f32[1,768]{1,0:T(1,128)} %get-tuple-element.97.gain_ref, ...), custom_call_target="tpu_custom_call" | custom-call | flops 1204224000 | bytes 4915200 | tf_op jit(solution)/shard_map/conv_norm/pallas_call | solution.py:91
  61.5 2.5 copy.64
  64.0 0.7 pad.29.index_ref
  64.7 0.7 pad.30.weight_ref
  65.4 0.5 pad_bitcast_fusion.place_ref
  65.9 0.7 pad_convert_fusion.cell_mask_ref
  66.6 11.9 %widen.1 = (bf16[800,3072]{1,0:T(8,128)(2,1)}, bf16[800,3072]{1,0:T(8,128)(2,1)}) custom-call(bf16[800,768]{1,0:T(8,128)(2,1)} %get-tuple-element.30.normed_ref, bf16[768,3072]{1,0:T(8,128)(2,1)} %all-gather.5.cloned.1.call-done.weight_ref, f32[1,3072]{1,0:T(1,128)} %convert.6.bias_ref), custom_call_target="tpu_custom_call" | custom-call | flops 7549747200 | bytes 15777792 | tf_op jit(solution)/shard_map/widen/pallas_call | solution.py:125
  78.6 38.9 %all-gather.7.cloned.1.call-done.weight_ref = bf16[3072,768]{1,0:T(8,128)(2,1)} async-done(((bf16[384,768]{1,0:T(8,128)(2,1)}), bf16[3072,768]{1,0:T(8,128)(2,1)}) %all-gather.7.cloned.1.call-update) | async-done | bytes 4718608 | tf_op jit(solution)/shard_map/all_gather | solution.py:525
  117.4 9.9 %narrow.1.branch_ref = f32[800,768]{1,0:T(8,128)} custom-call(bf16[800,3072]{1,0:T(8,128)(2,1)} %get-tuple-element.31.active_ref, bf16[3072,768]{1,0:T(8,128)(2,1)} %all-gather.7.cloned.1.call-done.weight_ref, f32[1,768]{1,0:T(1,128)} %get-tuple-element.95.bias_ref), custom_call_target="tpu_custom_call" | custom-call | flops 3774873600 | bytes 12091392 | tf_op jit(solution)/shard_map/narrow/pallas_call | solution.py:156
  127.4 14.2 %flow.1 = (bf16[4,2,100,768]{3,2,1,0:T(8,128)(2,1)}, f32[800,768]{1,0:T(8,128)}, bf16[800,768]{1,0:T(8,128)(2,1)}, f32[1,768]{1,0:T(1,128)}, f32[1,768]{1,0:T(1,128)}, /*index=5*/f32[128,768]{1,0:T(8,128)}) custom-call(bf16[800,768]{1,0:T(8,128)(2,1)} %reshape.138.x_ref, f32[800,768]{1,0:T(8,128)} %narrow.1.branch_ref, ...), custom_call_target="tpu_custom_call" | custom-call | flops 4000000000 | bytes 9830400 | tf_op jit(solution)/shard_map/flow/pallas_call | solution.py:304
  141.6 16.9 %hidden_back.1 = (bf16[800,3072]{1,0:T(8,128)(2,1)}, f32[1,3072]{1,0:T(1,128)}, bf16[8,768,384]{2,1,0:T(8,128)(2,1)}) custom-call(bf16[800,768]{1,0:T(8,128)(2,1)} %get-tuple-element.33.dbranch_ref, bf16[3072,768]{1,0:T(8,128)(2,1)} %all-gather.7.cloned.1.call-done.weight_ref, bf16[800,3072]{1,0:T(8,128)(2,1)} %get-tuple-element.34.slope_ref, ...), custom_call_target="tpu_custom_call" | custom-call | flops 7549747200 | bytes 24182784 | tf_op jit(solution)/shard_map/hidden_back/pallas_call | solution.py:356
  158.4 11.9 %norm_back.1 = (f32[800,768]{1,0:T(8,128)}, f32[1,768]{1,0:T(1,128)}, f32[1,768]{1,0:T(1,128)}, f32[1,768]{1,0:T(1,128)}) custom-call(bf16[800,3072]{1,0:T(8,128)(2,1)} %get-tuple-element.35.dhidden_ref, bf16[768,3072]{1,0:T(8,128)(2,1)} %all-gather.5.cloned.1.call-done.weight_ref, f32[800,768]{1,0:T(8,128)} %get-tuple-element.36.xhat_ref, ...), custom_call_target="tpu_custom_call" | custom-call | flops 3774873600 | bytes 14548992 | tf_op jit(solution)/shard_map/norm_back/pallas_call | solution.py:421
  170.4 10.4 %grad_taps.1 = f32[49,768]{1,0:T(8,128)} custom-call(bf16[800,768]{1,0:T(8,128)(2,1)} %reshape.138.x_ref, f32[100,8,768]{2,1,0:T(8,128)} %bitcast.59), custom_call_target="tpu_custom_call" | custom-call | flops 1204224000 | bytes 3686400 | tf_op jit(solution)/shard_map/grad_taps/pallas_call | solution.py:466
  180.9 1.3 concatenate.7
  182.2 1.1 copy.71
  183.4 30.4 %reduce-scatter.10.cloned.1.call-done = f32[96,182]{1,0:T(8,128)} async-done(((f32[768,182]{1,0:T(8,128)}), f32[96,182]{1,0:T(8,128)}) %reduce-scatter.10.cloned.1.call-update) | async-done | bytes 69904
  213.8 1.6 copy.72
  215.5 6.6 %copy.67 = bf16[768,8,384]{0,2,1:T(8,128)(2,1)} copy(bf16[768,8,384]{2,0,1:T(8,128)(2,1)} %bitcast.55) | data formatting | bytes 9437184 | tf_op jit(solution)/shard_map/transpose | solution.py:573
  222.2 6.6 %copy.73 = bf16[768,3072]{1,0:T(8,128)(2,1)} copy(bf16[768,3072]{0,1:T(8,128)(2,1)} %bitcast.54) | data formatting | bytes 9437184
  228.8 1.2 copy-done.1
  230.1 1.5 copy.68
  231.6 11.0 %grad_narrow.1 = bf16[8,768,384]{2,1,0:T(8,128)(2,1)} custom-call(bf16[768,800]{1,0:T(8,128)(2,1)} %bitcast.63, bf16[800,3072]{1,0:T(8,128)(2,1)} %get-tuple-element.31.active_ref), custom_call_target="tpu_custom_call" | custom-call | flops 3774873600 | bytes 10862592 | tf_op jit(solution)/shard_map/grad_narrow/pallas_call | solution.py:332
  242.6 6.6 %copy.69 = bf16[8,384,768]{2,1,0:T(8,128)(2,1)} copy(bf16[8,384,768]{1,2,0:T(8,128)(2,1)} %bitcast.56) | data formatting | bytes 9437184 | tf_op jit(solution)/shard_map/transpose | solution.py:572
  249.2 1.0 copy.65.mask_ref
  250.2 0.6 dynamic-slice
  251.5 2.0 copy.63
  253.5 11.8 %conv_back.1 = f32[100,8,768]{2,1,0:T(8,128)} custom-call(f32[100,8,768]{2,1,0:T(8,128)} %bitcast.60, f32[49,768]{1,0:T(8,128)} %slice_convert_fusion.kernel_ref, f32[100,8,768]{2,1,0:T(8,128)} %bitcast.58, f32[100,8,1]{2,1,0:T(8,128)} %copy.65.mask_ref), custom_call_target="tpu_custom_call" | custom-call | flops 1204224000 | bytes 7372800 | tf_op jit(solution)/shard_map/conv_back/pallas_call | solution.py:492
  265.2 2.8 reshape.144
  268.0 2.7 copy.77
  270.8 28.0 %all-reduce.6 = f32[3072]{0:T(1024)S(1)} all-reduce(f32[3072]{0:T(1024)S(1)} %bitcast.75), channel_id=4, replica_groups=mesh['dp'=4,'fsdp'=8] {'fsdp'}, use_global_device_ids=true, to_apply=%region_4.5.clone | all-reduce | flops 3072 | bytes 24576
  298.8 0.9 slice.84
  299.7 0.6 gather_fusion
  300.3 1.4 slice.78
  301.6 1.4 slice_bitcast_fusion
  303.0 0.7 broadcast_select_fusion.1
  303.7 11.6 %reduce-scatter.12.cloned.1.call-done = bf16[96,3072]{1,0:T(8,128)(2,1)} async-done(((bf16[768,3072]{1,0:T(8,128)(2,1)}), bf16[96,3072]{1,0:T(8,128)(2,1)}) %reduce-scatter.12.cloned.1.call-update) | async-done | bytes 589840
  315.3 1.4 copy.74
  316.7 54.1 %reduce-scatter.8.cloned.1.call-done = bf16[384,768]{1,0:T(8,128)(2,1)} async-done(((bf16[3072,768]{1,0:T(8,128)(2,1)}), bf16[384,768]{1,0:T(8,128)(2,1)}) %reduce-scatter.8.cloned.1.call-update) | async-done | bytes 589840 | tf_op jit(solution)/shard_map/reduce_scatter | solution.py:570
  370.8 94.6 %all-reduce.12 = (f32[96,3072]{0,1:T(8,128)S(1)}, f32[384]{0:T(512)}, f32[384,768]{1,0:T(8,128)}) all-reduce(bf16[96,3072]{0,1:T(8,128)(2,1)S(1)} %copy.74, f32[384]{0:T(512)S(1)} %dynamic-slice.1, bf16[384,768]{1,0:T(8,128)(2,1)} %reduce-scatter.8.cloned.1.call-done), channel_id=1, replica_groups=mesh['dp'=4,'fsdp'=8] {'dp'}, use_global_device_ids=true, to_apply=%region_3.4 | all-reduce | flops 590208 | bytes 3542016 | tf_op jit(solution)/shard_map/psum | solution.py:570
  465.4 1.5 copy.70
  (66 shorter events, 0.7 us)
Async XLA Ops:
  7.2 2.4 copy-start.2
  7.2 59.5 %all-gather.5.cloned.1.call-start = ((), (), s32[]{:S(2)}) async-start(), calls=%async_computation.3 | async-start | bytes 5308416 | tf_op jit(solution)/shard_map/all_gather | solution.py:525
  7.9 109.5 %all-gather.7.cloned.1.call-start = ((), (), s32[]{:S(2)}) async-start(), calls=%async_computation.4 | async-start | bytes 5308416 | tf_op jit(solution)/shard_map/all_gather | solution.py:525
  8.7 205.2 %reduce-scatter.10.cloned.1.call-start = ((), (), s32[]{:S(2)}) async-start(), calls=%async_computation.7 | async-start | bytes 884736
  11.4 1.3 copy-start.5
  11.4 1.3 copy-start.6
  11.4 1.3 copy-start.17
  11.4 1.3 copy-start.18
  11.4 1.3 copy-start.19
  11.4 1.3 copy-start.20
  11.4 1.3 copy-start.21
  11.5 18.6 %copy-start.15 = (bf16[384]{0:T(512)(128)(2,1)S(1)}, bf16[384]{0:T(512)(128)(2,1)}, u32[]{:S(2)}) copy-start(bf16[384]{0:T(512)(128)(2,1)} %param.28) | copy-start | bytes 2308
  12.7 32.5 %copy-start.3 = (bf16[4,2,10,10,768]{4,1,3,2,0:T(2,128)(2,1)S(1)}, bf16[4,2,10,10,768]{4,1,3,2,0:T(2,128)(2,1)}, u32[]{:S(2)}) copy-start(bf16[4,2,10,10,768]{4,1,3,2,0:T(2,128)(2,1)} %param.18) | copy-start | bytes 3686404
  45.0 0.7 copy-start.8
  45.1 0.7 copy-start.9
  61.5 3.9 copy-start.16
  170.3 10.5 %copy-start.4 = (f32[128,768]{1,0:T(8,128)S(1)}, f32[128,768]{1,0:T(8,128)}, u32[]{:S(2)}) copy-start(f32[128,768]{1,0:T(8,128)} %get-tuple-element.45) | copy-start | bytes 1179652
  170.3 10.5 %copy-start.10 = (f32[1,768]{1,0:T(1,128)S(1)}, f32[1,768]{1,0:T(1,128)}, u32[]{:S(2)}) copy-start(f32[1,768]{1,0:T(1,128)} %get-tuple-element.44) | copy-start | bytes 9220
  170.3 10.5 %copy-start.11 = (f32[1,768]{1,0:T(1,128)S(1)}, f32[1,768]{1,0:T(1,128)}, u32[]{:S(2)}) copy-start(f32[1,768]{1,0:T(1,128)} %get-tuple-element.43) | copy-start | bytes 9220
  170.4 10.5 %copy-start.12 = (f32[1,768]{1,0:T(1,128)S(1)}, f32[1,768]{1,0:T(1,128)}, u32[]{:S(2)}) copy-start(f32[1,768]{1,0:T(1,128)} %get-tuple-element.41) | copy-start | bytes 9220
  170.4 10.5 %copy-start.13 = (f32[1,768]{1,0:T(1,128)S(1)}, f32[1,768]{1,0:T(1,128)}, u32[]{:S(2)}) copy-start(f32[1,768]{1,0:T(1,128)} %get-tuple-element.42) | copy-start | bytes 9220
  170.4 10.5 %copy-start.14 = (f32[1,768]{1,0:T(1,128)S(1)}, f32[1,768]{1,0:T(1,128)}, u32[]{:S(2)}) copy-start(f32[1,768]{1,0:T(1,128)} %get-tuple-element.40) | copy-start | bytes 9220
  183.4 115.4 %all-reduce.11.cloned.1.call-start = ((), (), s32[]{:S(2)}) async-start(), calls=%async_computation.5 | async-start | bytes 188416 | tf_op jit(solution)/shard_map/psum | solution.py:570
  215.5 99.8 %reduce-scatter.12.cloned.1.call-start = ((), (), s32[]{:S(2)}) async-start(), calls=%async_computation.8 | async-start | bytes 5308416
  228.8 1.3 copy-start.1
  228.8 142.0 %reduce-scatter.8.cloned.1.call-start = ((), (), s32[]{:S(2)}) async-start(), calls=%async_computation.6 | async-start | bytes 5308416 | tf_op jit(solution)/shard_map/reduce_scatter | solution.py:570
  249.2 1.0 copy-start.22
  249.2 2.3 copy-start
  268.0 2.7 copy-start.7
Sparse Core Ops, SparseCore 0:
  9.7 55.4 all-gather.4
  66.8 50.5 all-gather.6
  183.5 30.2 reduce-scatter.9
  217.4 40.0 all-reduce.10
  259.6 55.6 reduce-scatter.11
  317.5 53.3 reduce-scatter.7
